TPU v7x, 32 devices: a whole 2x2x4 slice. The times are simulated.
32 devices in a mesh: seq: 4 (over y, x), chan: 8 (over z, core).
Axes of the slice: x: 2, y: 2, z: 4, core: 2. Of those that a mesh axis runs over, the one named last changes fastest.
Arguments:
- signal: float32 [2048, 4096], P('seq', 'chan'), may hold values from -6 to 6
- filter_taps: float32 [2048, 4096], P('seq', 'chan'), may hold values from -3 to 3
- out_gate: float32 [2048, 4096], P('seq', 'chan'), may hold values from -6 to 6
- skip_gain: float32 [4096], P('chan'), may hold values from -4 to 4
- lengths: int32 [32], replicated, may hold values from 1 to 512, 2048 in all
- row_of_segment: int32 [32], replicated, may hold values from 0 to 31, each once
Outputs:
- mixed: float32 [2048, 4096], P('seq', 'chan')
- pooled: float32 [32, 4096], P('seq', 'chan')
Inputs may be any that keep to these rules, and one draw needn't show every extreme that they name: `lengths`: segments tile the sequence; pooled row r belongs to index r // 8 of seq. `row_of_segment`: each row appears once.
All inputs are finite; a program needn't handle non-finite values.
Results may differ from a plain program's by a relative error of at most 0.000078.
Values sent between devices are 32-bit elements; how exact they have to be, the bound alone decides.
A program may use at most 64 MiB of HBM per device.

v0:
```python
import functools
import math

import jax
import jax.numpy as jnp
import ml_dtypes
import numpy as np
from jax import lax
from jax.experimental import pallas as pl
from jax.experimental.pallas import tpu as pltpu
from jax.sharding import PartitionSpec as P

LANES = 128
MESH = pl.DeviceIdType.MESH

exact_mode = lax.Precision.HIGHEST


def complex_dot(left_re, left_im, right_re, right_im):
    out_re = jnp.dot(left_re, right_re, precision=exact_mode) - jnp.dot(
        left_im, right_im, precision=exact_mode
    )
    out_im = jnp.dot(left_re, right_im, precision=exact_mode) + jnp.dot(
        left_im, right_re, precision=exact_mode
    )
    return (out_re, out_im)


def rotate(real_part, imag_part, phase_angle):
    cosine = jnp.cos(phase_angle)
    sine = jnp.sin(phase_angle)
    return (real_part * cosine - imag_part * sine, real_part * sine + imag_part * cosine)


def local_transform(real_part, imag_part, direction):
    block_rows, columns = real_part.shape
    outer_size = max(
        (divisor for divisor in range(1, math.isqrt(block_rows) + 1) if block_rows % divisor == 0)
    )
    inner_size = block_rows // outer_size
    outer_index = jnp.arange(outer_size, dtype=jnp.int32)
    inner_index = jnp.arange(inner_size, dtype=jnp.int32)
    outer_angle = (
        direction
        * 2.0
        * math.pi
        * (outer_index[:, None] * outer_index[None, :] % outer_size).astype(jnp.float32)
        / outer_size
    )
    twist_angle = (
        direction
        * 2.0
        * math.pi
        * (outer_index[:, None] * inner_index[None, :] % block_rows).astype(jnp.float32)
        / block_rows
    )
    inner_angle = (
        direction
        * 2.0
        * math.pi
        * (inner_index[:, None] * inner_index[None, :] % inner_size).astype(jnp.float32)
        / inner_size
    )
    step_re, step_im = complex_dot(
        jnp.cos(outer_angle),
        jnp.sin(outer_angle),
        real_part.reshape(outer_size, inner_size * columns),
        imag_part.reshape(outer_size, inner_size * columns),
    )
    step_re = step_re.reshape(outer_size, inner_size, columns)
    step_im = step_im.reshape(outer_size, inner_size, columns)
    step_re, step_im = rotate(step_re, step_im, twist_angle[:, :, None])
    inner_cos = jnp.cos(inner_angle)
    inner_sin = jnp.sin(inner_angle)
    out_re = jnp.einsum("sak,at->tsk", step_re, inner_cos, precision=exact_mode) - jnp.einsum(
        "sak,at->tsk", step_im, inner_sin, precision=exact_mode
    )
    out_im = jnp.einsum("sak,at->tsk", step_re, inner_sin, precision=exact_mode) + jnp.einsum(
        "sak,at->tsk", step_im, inner_cos, precision=exact_mode
    )
    return (out_re.reshape(block_rows, columns), out_im.reshape(block_rows, columns))


def convolve_channels(signal, filter_taps):
    signal_cols, taps_cols = (
        lax.all_to_all(signal, "seq", split_axis=1, concat_axis=0, tiled=True),
        lax.all_to_all(filter_taps, "seq", split_axis=1, concat_axis=0, tiled=True),
    )
    total_rows, width = signal_cols.shape
    joined = jnp.concatenate((signal_cols, taps_cols), axis=1)
    padded = jnp.concatenate((joined, jnp.zeros_like(joined)), axis=0)
    spec_re, spec_im = local_transform(padded, jnp.zeros_like(padded), -1.0)
    left_re, left_im = (spec_re[:, :width], spec_im[:, :width])
    right_re, right_im = (spec_re[:, width:], spec_im[:, width:])
    product_re = left_re * right_re - left_im * right_im
    product_im = left_re * right_im + left_im * right_re
    back_re, back_im = local_transform(product_re, product_im, 1.0)
    conv_cols = back_re[:total_rows] / (2.0 * total_rows)
    return lax.all_to_all(conv_cols, "seq", split_axis=0, concat_axis=1, tiled=True)


def pool_segments(mixed, lengths, row_of_segment, seq_index, seq_count):
    block_rows = mixed.shape[0]
    owned_rows = lengths.shape[0] // seq_count
    span_ends = jnp.cumsum(lengths)
    span_starts = span_ends - lengths
    tokens = seq_index * block_rows + jnp.arange(block_rows, dtype=jnp.int32)
    inside = (span_starts[None, :] <= tokens[:, None]) & (tokens[:, None] < span_ends[None, :])
    token_row = jnp.sum(jnp.where(inside, row_of_segment[None, :], 0), axis=1)
    wanted = jnp.arange(owned_rows * lax.axis_size("seq"), dtype=jnp.int32)
    member = (token_row[None, :] == wanted[:, None]).astype(jnp.float32)
    sums = lax.psum_scatter(
        jnp.dot(member, mixed, precision=exact_mode), "seq", scatter_dimension=0, tiled=True
    )
    mine = seq_index * owned_rows + jnp.arange(owned_rows, dtype=jnp.int32)
    seg_sizes = jnp.sum(
        jnp.where(row_of_segment[None, :] == mine[:, None], lengths[None, :], 0), axis=1
    )
    return sums / seg_sizes.astype(jnp.float32)[:, None]


def split_constant(table):
    high = table.astype(np.float32).astype(ml_dtypes.bfloat16)
    low = (table - high.astype(np.float64)).astype(np.float32).astype(ml_dtypes.bfloat16)
    return np.stack([high, low])


def transform_tables(block):
    freqs = np.concatenate([np.arange(0, block, 2), np.arange(1, block, 2)])
    turns = ((2 * freqs[:, None] + 1) * np.arange(block)[None, :]) % (4 * block)
    angle = turns * (np.pi / (2 * block))
    forward = np.concatenate([np.cos(angle), -np.sin(angle)], axis=0)
    inverse = forward.T / block
    return split_constant(forward), split_constant(inverse)


def split_value(value):
    high = value.astype(jnp.bfloat16)
    low = (value - high.astype(jnp.float32)).astype(jnp.bfloat16)
    return high, low


def mul(left, right):
    return jnp.dot(left, right, preferred_element_type=jnp.float32)


def peer_of(me, offset, count):
    peer, place = 0, 1
    while place < count:
        peer = peer + ((me // place + offset // place) % 2) * place
        place *= 2
    return peer


def mixer_kernel(
    count, block,
    lengths, rows, signal, taps, gate, skip, forward, inverse,
    mixed, pooled,
    sig_in, tap_in, sig_own, gate_own, spec_s, spec_h, prod, conv_out, conv_in, mixed_v, member, part, part_in,
    fwd_v, inv_v,
    local_sem, table_sem, gate_sem, tap_sem, send_s, recv_s, send_h, recv_h, send_c, recv_c, send_p, recv_p, out_sem,
):
    me = lax.axis_index("seq")
    tokens, width = signal.shape
    lanes = width // count
    halves = tokens // block
    blocks = halves * count
    owned = part.shape[1]
    segs = owned * count
    peers = [peer_of(me, d, count) for d in range(count)]

    def cols(index):
        return pl.ds(pl.multiple_of(index * lanes, LANES), lanes)

    fwd_copy = pltpu.make_async_copy(forward, fwd_v, table_sem.at[0])
    inv_copy = pltpu.make_async_copy(inverse, inv_v, table_sem.at[1])
    tap_copy = pltpu.make_async_copy(taps.at[:, cols(me)], tap_in.at[0], tap_sem)
    sig_copies = [
        pltpu.make_async_copy(signal.at[:, cols(peers[d])], sig_own.at[d], local_sem.at[d]) for d in range(count)
    ]
    gate_copies = [
        pltpu.make_async_copy(gate.at[:, cols(peers[d])], gate_own.at[d], gate_sem.at[d]) for d in range(count)
    ]

    barrier = pltpu.get_barrier_semaphore()
    for d in range(1, count):
        pl.semaphore_signal(barrier, inc=1, device_id={"seq": peers[d]}, device_id_type=MESH)
    fwd_copy.start()
    sig_copies[0].start()
    tap_copy.start()
    pl.semaphore_wait(barrier, count - 1)

    def remote(src, dst, send, recv, d):
        return pltpu.make_async_remote_copy(
            src_ref=src, dst_ref=dst, send_sem=send.at[d], recv_sem=recv.at[d],
            device_id={"seq": peers[d]}, device_id_type=MESH,
        )

    order = list(range(count - 1, 0, -1))
    sig_sends = {d: remote(signal.at[:, cols(peers[d])], sig_in.at[d], send_s, recv_s, d) for d in order}
    tap_sends = {d: remote(taps.at[:, cols(peers[d])], tap_in.at[d], send_h, recv_h, d) for d in order}
    for d in order:
        sig_sends[d].start()
    for d in order:
        tap_sends[d].start()
    inv_copy.start()
    for d in range(1, count):
        sig_copies[d].start()
    for d in range(count):
        gate_copies[d].start()

    token = me * tokens + lax.broadcasted_iota(jnp.int32, (8, tokens), 1)
    mine = me * owned + lax.broadcasted_iota(jnp.int32, (owned, LANES), 0)
    start = jnp.int32(0)
    token_row = jnp.zeros((8, tokens), jnp.int32)
    sizes = jnp.zeros((owned, LANES), jnp.int32)
    for k in range(segs):
        stop = start + lengths[k]
        token_row = jnp.where((token >= start) & (token < stop), rows[k], token_row)
        sizes = jnp.where(mine == rows[k], lengths[k], sizes)
        start = stop
    row_at = lax.broadcasted_iota(jnp.int32, (segs, tokens), 0)
    member[...] = (row_at == token_row[0:1, :]).astype(jnp.float32).astype(jnp.bfloat16)

    fwd_copy.wait()

    def to_spectrum(source, place, spec):
        value = source[...]
        wide = jnp.concatenate([value[h * block:(h + 1) * block] for h in range(halves)], axis=1)
        high, low = split_value(wide)
        result = mul(fwd_v[0], high) + (mul(fwd_v[1], high) + mul(fwd_v[0], low))
        for h in range(halves):
            spec[place * halves + h] = result[:, h * lanes:(h + 1) * lanes]

    sig_copies[0].wait()
    to_spectrum(sig_own.at[0], me, spec_s)
    tap_copy.wait()
    to_spectrum(tap_in.at[0], me, spec_h)
    for d in order[::-1]:
        sig_sends[d].wait_recv()
        to_spectrum(sig_in.at[d], peers[d], spec_s)
    for d in order[::-1]:
        tap_sends[d].wait_recv()
        to_spectrum(tap_in.at[d], peers[d], spec_h)

    def product_tile(sign, row):
        re = pl.ds(pl.multiple_of(row, 8), 8)
        im = pl.ds(pl.multiple_of(row + block, 8), 8)
        s_re = [spec_s[i, re, :] for i in range(blocks)]
        s_im = [spec_s[i, im, :] for i in range(blocks)]
        h_re = [spec_h[i, re, :] for i in range(blocks)]
        h_im = [spec_h[i, im, :] for i in range(blocks)]
        old_re = old_im = None
        for j in range(blocks):
            new_re = new_im = None
            for i in range(j + 1):
                k = j - i
                a = s_re[i] * h_re[k] - s_im[i] * h_im[k]
                b = s_re[i] * h_im[k] + s_im[i] * h_re[k]
                new_re = a if new_re is None else new_re + a
                new_im = b if new_im is None else new_im + b
            out_re, out_im = new_re, new_im
            if j:
                out_re = new_re - old_im if sign > 0 else new_re + old_im
                out_im = new_im + old_re if sign > 0 else new_im - old_re
            at = pl.ds((j % halves) * lanes, lanes)
            prod[j // halves, re, at] = out_re
            prod[j // halves, im, at] = out_im
            old_re, old_im = new_re, new_im

    steps = block // 16
    for sign, base in ((1, 0), (-1, block // 2)):
        def body(t, carry, sign=sign, base=base):
            product_tile(sign, base + t * 8)
            return carry
        lax.fori_loop(0, steps, body, 0)

    inv_copy.wait()

    def from_spectrum(place, target):
        high, low = split_value(prod[place])
        result = mul(inv_v[0], high) + (mul(inv_v[1], high) + mul(inv_v[0], low))
        for h in range(halves):
            target[h * block:(h + 1) * block, :] = result[:, h * lanes:(h + 1) * lanes]

    conv_sends = {d: remote(conv_out.at[d], conv_in.at[d], send_c, recv_c, d) for d in order}
    for d in order:
        from_spectrum(peers[d], conv_out.at[d])
        conv_sends[d].start()
    from_spectrum(me, conv_out.at[0])

    out_copies = []

    def finish(d, conv):
        sig_copies[d].wait() if d else None
        gate_copies[d].wait()
        gain = skip[0:1, cols(peers[d])]
        value = gate_own[d] * (conv[...] + gain * sig_own[d])
        mixed_v[d] = value
        copy = pltpu.make_async_copy(mixed_v.at[d], mixed.at[:, cols(peers[d])], out_sem.at[d])
        copy.start()
        out_copies.append(copy)
        high, low = split_value(value)
        sums = mul(member[...], high) + mul(member[...], low)
        for p in range(count):
            part[p, :, cols(peers[d])] = sums[p * owned:(p + 1) * owned]

    finish(0, conv_out.at[0])
    for d in order[::-1]:
        conv_sends[d].wait_recv()
        finish(d, conv_in.at[d])

    part_sends = {d: remote(part.at[peers[d]], part_in.at[d], send_p, recv_p, d) for d in order}
    for d in order:
        part_sends[d].start()
    total = part[me]
    for d in order:
        part_sends[d].wait_recv()
        total = total + part_in[d]
    pooled[...] = total / jnp.concatenate([sizes] * (width // LANES), axis=1).astype(jnp.float32)

    for copy in out_copies:
        copy.wait()
    for group in (sig_sends, tap_sends, conv_sends, part_sends):
        for d in order:
            group[d].wait_send()


def fits_kernel(tokens, width, count):
    return (
        count > 1
        and count & (count - 1) == 0
        and width % (count * LANES) == 0
        and tokens % (2 * LANES) == 0
    )


def fused_on_device(count, signal, filter_taps, out_gate, skip_gain, lengths, row_of_segment):
    tokens, width = signal.shape
    lanes = width // count
    block = 2 * LANES
    halves = tokens // block
    owned = lengths.shape[0] // count
    segs = owned * count
    forward, inverse = transform_tables(block)
    f32, bf16 = jnp.float32, jnp.bfloat16
    dma = pltpu.SemaphoreType.DMA
    anywhere = pl.BlockSpec(memory_space=pl.ANY)
    scalars = pl.BlockSpec(memory_space=pltpu.SMEM)
    vmem = pl.BlockSpec(memory_space=pltpu.VMEM)
    piece = pltpu.VMEM((count, tokens, lanes), f32)
    spectra = pltpu.VMEM((count * halves, 2 * block, lanes), f32)
    return pl.pallas_call(
        functools.partial(mixer_kernel, count, block),
        out_shape=(
            jax.ShapeDtypeStruct((tokens, width), f32),
            jax.ShapeDtypeStruct((owned, width), f32),
        ),
        in_specs=[scalars, scalars, anywhere, anywhere, anywhere, vmem, anywhere, anywhere],
        out_specs=(anywhere, vmem),
        scratch_shapes=[
            piece, piece, piece, piece, spectra, spectra,
            pltpu.VMEM((count, 2 * block, halves * lanes), f32),
            piece, piece, piece,
            pltpu.VMEM((segs, tokens), bf16),
            pltpu.VMEM((count, owned, width), f32),
            pltpu.VMEM((count, owned, width), f32),
            pltpu.VMEM(forward.shape, bf16),
            pltpu.VMEM(inverse.shape, bf16),
            dma((count,)), dma((2,)), dma((count,)), dma,
            dma((count,)), dma((count,)), dma((count,)), dma((count,)),
            dma((count,)), dma((count,)), dma((count,)), dma((count,)),
            dma((count,)),
        ],
        compiler_params=pltpu.CompilerParams(
            collective_id=0, has_side_effects=True, vmem_limit_bytes=40 * 1024 * 1024
        ),
        name="mixer",
    )(
        lengths, row_of_segment, signal, filter_taps, out_gate, skip_gain[None, :],
        jnp.asarray(forward), jnp.asarray(inverse),
    )


def on_device(signal, filter_taps, out_gate, skip_gain, lengths, row_of_segment):
    seq_count = lax.axis_size("seq")
    if fits_kernel(signal.shape[0], signal.shape[1], seq_count):
        return fused_on_device(
            seq_count, signal, filter_taps, out_gate, skip_gain, lengths, row_of_segment
        )
    seq_index = lax.axis_index("seq")
    conv = convolve_channels(signal, filter_taps)
    mixed = out_gate * (conv + skip_gain[None, :] * signal)
    pooled = pool_segments(mixed, lengths, row_of_segment, seq_index, seq_count)
    return (mixed, pooled)


def solution(mesh):
    placed = (P("seq", "chan"), P("seq", "chan"), P("seq", "chan"), P("chan"), P(), P())
    return jax.shard_map(
        on_device,
        mesh=mesh,
        in_specs=placed,
        out_specs=(P("seq", "chan"), P("seq", "chan")),
        check_vma=False,
    )
```

profile of v0, /device:TPU:0, one launch (start us, length us, event | category | flops | bytes accessed | tf_op | source)
XLA Modules:
  0.0 58.4 jit_solution(6528524898599815472)
XLA Ops:
  0.6 0.0 copy-start.7
  0.6 0.0 copy-start.6
  0.7 0.6 %copy-done.7 = s32[32]{0:T(128)S(1)} copy-done((s32[32]{0:T(128)S(1)}, s32[32]{0:T(128)}, u32[]{:S(2)}) %copy-start.7) | copy-done | bytes 152
  1.3 0.0 copy-done.6
  1.3 0.0 copy-start
  1.3 1.2 %copy-done = f32[512,512]{1,0:T(8,128)S(1)} copy-done((f32[512,512]{1,0:T(8,128)S(1)}, f32[512,512]{1,0:T(8,128)}, u32[]{:S(2)}) %copy-start) | copy-done | bytes 1048600
  2.5 0.0 copy-start.1
  2.5 1.2 %copy-done.1 = f32[512,512]{1,0:T(8,128)S(1)} copy-done((f32[512,512]{1,0:T(8,128)S(1)}, f32[512,512]{1,0:T(8,128)}, u32[]{:S(2)}) %copy-start.1) | copy-done | bytes 1048600
  3.8 0.0 copy-start.2
  3.8 1.2 %copy-done.2 = f32[512,512]{1,0:T(8,128)S(1)} copy-done((f32[512,512]{1,0:T(8,128)S(1)}, f32[512,512]{1,0:T(8,128)}, u32[]{:S(2)}) %copy-start.2) | copy-done | bytes 1048600
  5.0 0.0 copy-start.3
  5.0 1.0 %copy-done.3 = bf16[2,256,512]{2,1,0:T(8,128)(2,1)S(1)} copy-done((bf16[2,256,512]{2,1,0:T(8,128)(2,1)S(1)}, bf16[2,256,512]{2,1,0:T(8,128)(2,1)}, u32[]{:S(2)}) %copy-start.3) | copy-done | bytes 524312
  6.0 0.0 copy-start.4
  6.0 1.0 %copy-done.4 = bf16[2,512,256]{2,1,0:T(8,128)(2,1)S(1)} copy-done((bf16[2,512,256]{2,1,0:T(8,128)(2,1)S(1)}, bf16[2,512,256]{2,1,0:T(8,128)(2,1)}, u32[]{:S(2)}) %copy-start.4) | copy-done | bytes 524312
  7.1 0.0 copy-start.5
  7.1 0.7 %copy-done.5 = f32[512]{0:T(512)S(1)} copy-done((f32[512]{0:T(512)S(1)}, f32[512]{0:T(512)}, u32[]{:S(2)}) %copy-start.5) | copy-done | bytes 2072
  7.7 49.1 %mixer.1 = (f32[512,512]{1,0:T(8,128)S(1)}, f32[8,512]{1,0:T(8,128)S(1)}) custom-call(s32[32]{0:T(128)S(1)} %copy-done.6, s32[32]{0:T(128)S(1)} %copy-done.7, f32[512,512]{1,0:T(8,128)S(1)} %copy-done, f32[512,512]{1,0:T(8,128)S(1)} %copy-done.1, f32[512,512]{1,0:T(8,128)S(1)} %copy-done.2, f32[1,512]{1,0:T(1,128)S(1)} %bitcast.1, ...), custom_call_target="tpu_custom_call" | custom-call | tf_op jit(solution)/shard_map/mixer/pallas_call | solution.py:353
  56.8 1.0 %copy.12 = f32[512,512]{1,0:T(8,128)} copy(f32[512,512]{1,0:T(8,128)S(1)} %get-tuple-element.4) | data formatting | bytes 2097152
  57.8 0.6 %copy.13 = f32[8,512]{1,0:T(8,128)} copy(f32[8,512]{1,0:T(8,128)S(1)} %get-tuple-element.5) | data formatting | bytes 32768
Async XLA Ops:
  0.6 0.7 %copy-start.7 = (s32[32]{0:T(128)S(1)}, s32[32]{0:T(128)}, u32[]{:S(2)}) copy-start(s32[32]{0:T(128)} %rows.1) | copy-start | bytes 388
  0.6 0.7 %copy-start.6 = (s32[32]{0:T(128)S(1)}, s32[32]{0:T(128)}, u32[]{:S(2)}) copy-start(s32[32]{0:T(128)} %lengths.1) | copy-start | bytes 388
  1.3 1.2 %copy-start = (f32[512,512]{1,0:T(8,128)S(1)}, f32[512,512]{1,0:T(8,128)}, u32[]{:S(2)}) copy-start(f32[512,512]{1,0:T(8,128)} %signal.1) | copy-start | bytes 3145732
  2.5 1.2 %copy-start.1 = (f32[512,512]{1,0:T(8,128)S(1)}, f32[512,512]{1,0:T(8,128)}, u32[]{:S(2)}) copy-start(f32[512,512]{1,0:T(8,128)} %taps.1) | copy-start | bytes 3145732
  3.8 1.2 %copy-start.2 = (f32[512,512]{1,0:T(8,128)S(1)}, f32[512,512]{1,0:T(8,128)}, u32[]{:S(2)}) copy-start(f32[512,512]{1,0:T(8,128)} %gate.1) | copy-start | bytes 3145732
  5.0 1.0 %copy-start.3 = (bf16[2,256,512]{2,1,0:T(8,128)(2,1)S(1)}, bf16[2,256,512]{2,1,0:T(8,128)(2,1)}, u32[]{:S(2)}) copy-start(bf16[2,256,512]{2,1,0:T(8,128)(2,1)} %constant.5.clone.inverse) | copy-start | bytes 1572868
  6.0 1.0 %copy-start.4 = (bf16[2,512,256]{2,1,0:T(8,128)(2,1)S(1)}, bf16[2,512,256]{2,1,0:T(8,128)(2,1)}, u32[]{:S(2)}) copy-start(bf16[2,512,256]{2,1,0:T(8,128)(2,1)} %constant.4.clone.forward) | copy-start | bytes 1572868
  7.1 0.7 %copy-start.5 = (f32[512]{0:T(512)S(1)}, f32[512]{0:T(512)}, u32[]{:S(2)}) copy-start(f32[512]{0:T(512)} %param.11) | copy-start | bytes 6148
where the time goes:
time: 58.8 us; the launch traced here: 58.4 us
  Pallas kernels  49.1 us (84%)
  local copies, waits for them, and re-layouts  8.67 us (15%)
  between operations  0.66 us (1%)
    pallas_call x1, Pallas kernels, fused_on_device(): pl.pallas_call(functools.partial(mixer_kernel, count, block), out_shape=(...  49.1 us
    unnamed x18, local copies, waits for them, and re-layouts  8.67 us

commit v1 on v0

--- a/solution.py
+++ b/solution.py
@@ -154,10 +154,10 @@
 
 def mixer_kernel(
     count, block,
-    lengths, rows, signal, taps, gate, skip, forward, inverse,
+    lengths_at, rows_at, signal, taps, gate, skip_at, forward, inverse,
     mixed, pooled,
-    sig_in, tap_in, sig_own, gate_own, spec_s, spec_h, prod, conv_out, conv_in, mixed_v, member, part, part_in,
-    fwd_v, inv_v,
+    sig_in, tap_in, sig_own, gate_own, spec_s, spec_h, prod, carry, conv_out, conv_in, mixed_v, member, part, part_in,
+    fwd_v, inv_v, lengths, rows, skip,
     local_sem, table_sem, gate_sem, tap_sem, send_s, recv_s, send_h, recv_h, send_c, recv_c, send_p, recv_p, out_sem,
 ):
     me = lax.axis_index("seq")
@@ -168,12 +168,18 @@
     owned = part.shape[1]
     segs = owned * count
     peers = [peer_of(me, d, count) for d in range(count)]
+    pieces = [pl.ds(h * block, block) for h in range(halves)]
 
     def cols(index):
         return pl.ds(pl.multiple_of(index * lanes, LANES), lanes)
 
-    fwd_copy = pltpu.make_async_copy(forward, fwd_v, table_sem.at[0])
-    inv_copy = pltpu.make_async_copy(inverse, inv_v, table_sem.at[1])
+    table_copies = [
+        pltpu.make_async_copy(source, target, table_sem.at[i])
+        for i, (source, target) in enumerate(
+            ((forward, fwd_v), (inverse, inv_v), (lengths_at, lengths), (rows_at, rows), (skip_at, skip))
+        )
+    ]
+    fwd_copy, inv_copy, len_copy, row_copy, skip_copy = table_copies
     tap_copy = pltpu.make_async_copy(taps.at[:, cols(me)], tap_in.at[0], tap_sem)
     sig_copies = [
         pltpu.make_async_copy(signal.at[:, cols(peers[d])], sig_own.at[d], local_sem.at[d]) for d in range(count)
@@ -188,27 +194,42 @@
     fwd_copy.start()
     sig_copies[0].start()
     tap_copy.start()
+    len_copy.start()
+    row_copy.start()
     pl.semaphore_wait(barrier, count - 1)
 
-    def remote(src, dst, send, recv, d):
+    def remote(src, dst, send, recv, peer):
         return pltpu.make_async_remote_copy(
-            src_ref=src, dst_ref=dst, send_sem=send.at[d], recv_sem=recv.at[d],
-            device_id={"seq": peers[d]}, device_id_type=MESH,
+            src_ref=src, dst_ref=dst, send_sem=send, recv_sem=recv,
+            device_id={"seq": peer}, device_id_type=MESH,
         )
 
+    def scatter(source, target, send, recv):
+        return {
+            (d, h): remote(
+                source.at[pieces[h], cols(peers[d])], target.at[d, pieces[h], :],
+                send.at[d, h], recv.at[d, h], peers[d],
+            )
+            for h in range(halves)
+            for d in order
+        }
+
     order = list(range(count - 1, 0, -1))
-    sig_sends = {d: remote(signal.at[:, cols(peers[d])], sig_in.at[d], send_s, recv_s, d) for d in order}
-    tap_sends = {d: remote(taps.at[:, cols(peers[d])], tap_in.at[d], send_h, recv_h, d) for d in order}
-    for d in order:
-        sig_sends[d].start()
-    for d in order:
-        tap_sends[d].start()
+    sig_sends = scatter(signal, sig_in, send_s, recv_s)
+    tap_sends = scatter(taps, tap_in, send_h, recv_h)
+    for copy in sig_sends.values():
+        copy.start()
+    for copy in tap_sends.values():
+        copy.start()
     inv_copy.start()
+    skip_copy.start()
     for d in range(1, count):
         sig_copies[d].start()
     for d in range(count):
         gate_copies[d].start()
 
+    len_copy.wait()
+    row_copy.wait()
     token = me * tokens + lax.broadcasted_iota(jnp.int32, (8, tokens), 1)
     mine = me * owned + lax.broadcasted_iota(jnp.int32, (owned, LANES), 0)
     start = jnp.int32(0)
@@ -236,22 +257,21 @@
     to_spectrum(sig_own.at[0], me, spec_s)
     tap_copy.wait()
     to_spectrum(tap_in.at[0], me, spec_h)
-    for d in order[::-1]:
-        sig_sends[d].wait_recv()
-        to_spectrum(sig_in.at[d], peers[d], spec_s)
-    for d in order[::-1]:
-        tap_sends[d].wait_recv()
-        to_spectrum(tap_in.at[d], peers[d], spec_h)
-
-    def product_tile(sign, row):
+    for sends, source, spec in ((sig_sends, sig_in, spec_s), (tap_sends, tap_in, spec_h)):
+        for d in order[::-1]:
+            for h in range(halves):
+                sends[d, h].wait_recv()
+            to_spectrum(source.at[d], peers[d], spec)
+
+    def product_tile(sign, row, first, last):
         re = pl.ds(pl.multiple_of(row, 8), 8)
         im = pl.ds(pl.multiple_of(row + block, 8), 8)
-        s_re = [spec_s[i, re, :] for i in range(blocks)]
-        s_im = [spec_s[i, im, :] for i in range(blocks)]
-        h_re = [spec_h[i, re, :] for i in range(blocks)]
-        h_im = [spec_h[i, im, :] for i in range(blocks)]
-        old_re = old_im = None
-        for j in range(blocks):
+        s_re = [spec_s[i, re, :] for i in range(last)]
+        s_im = [spec_s[i, im, :] for i in range(last)]
+        h_re = [spec_h[i, re, :] for i in range(last)]
+        h_im = [spec_h[i, im, :] for i in range(last)]
+        old_re, old_im = (carry[re, :], carry[im, :]) if first else (None, None)
+        for j in range(first, last):
             new_re = new_im = None
             for i in range(j + 1):
                 k = j - i
@@ -267,63 +287,86 @@
             prod[j // halves, re, at] = out_re
             prod[j // halves, im, at] = out_im
             old_re, old_im = new_re, new_im
-
-    steps = block // 16
-    for sign, base in ((1, 0), (-1, block // 2)):
-        def body(t, carry, sign=sign, base=base):
-            product_tile(sign, base + t * 8)
-            return carry
-        lax.fori_loop(0, steps, body, 0)
+        if last < blocks:
+            carry[re, :] = old_re
+            carry[im, :] = old_im
+
+    def products(first, last):
+        for sign, base in ((1, 0), (-1, block // 2)):
+            def body(t, state, sign=sign, base=base):
+                product_tile(sign, base + t * 8, first, last)
+                return state
+            lax.fori_loop(0, block // 16, body, 0)
+
+    def back_copy(d, h, peer):
+        return remote(
+            conv_out.at[d, pieces[h], :], conv_in.at[d, pieces[h], :], send_c.at[d, h], recv_c.at[d, h], peer
+        )
+
+    def give_back(owner):
+        high, low = split_value(prod[owner])
+        result = mul(inv_v[0], high) + (mul(inv_v[1], high) + mul(inv_v[0], low))
+        d = peer_of(me, owner, count)
+        for h in range(halves):
+            conv_out[d, pieces[h], :] = result[:, h * lanes:(h + 1) * lanes]
+
+        @pl.when(me != owner)
+        def _():
+            for h in range(halves):
+                back_copy(d, h, owner).start()
 
     inv_copy.wait()
-
-    def from_spectrum(place, target):
-        high, low = split_value(prod[place])
-        result = mul(inv_v[0], high) + (mul(inv_v[1], high) + mul(inv_v[0], low))
-        for h in range(halves):
-            target[h * block:(h + 1) * block, :] = result[:, h * lanes:(h + 1) * lanes]
-
-    conv_sends = {d: remote(conv_out.at[d], conv_in.at[d], send_c, recv_c, d) for d in order}
-    for d in order:
-        from_spectrum(peers[d], conv_out.at[d])
-        conv_sends[d].start()
-    from_spectrum(me, conv_out.at[0])
+    products(0, blocks // 2)
+    for owner in range(count // 2):
+        give_back(owner)
+    products(blocks // 2, blocks)
+    for owner in range(count // 2, count):
+        give_back(owner)
 
     out_copies = []
 
-    def finish(d, conv):
-        sig_copies[d].wait() if d else None
-        gate_copies[d].wait()
-        gain = skip[0:1, cols(peers[d])]
-        value = gate_own[d] * (conv[...] + gain * sig_own[d])
-        mixed_v[d] = value
-        copy = pltpu.make_async_copy(mixed_v.at[d], mixed.at[:, cols(peers[d])], out_sem.at[d])
+    def finish(d, h, conv):
+        at = cols(peers[d])
+        value = gate_own[d, pieces[h], :] * (conv[d, pieces[h], :] + skip[:, at] * sig_own[d, pieces[h], :])
+        mixed_v[d, pieces[h], :] = value
+        copy = pltpu.make_async_copy(mixed_v.at[d, pieces[h], :], mixed.at[pieces[h], at], out_sem.at[d, h])
         copy.start()
         out_copies.append(copy)
         high, low = split_value(value)
-        sums = mul(member[...], high) + mul(member[...], low)
+        inside = member[:, h * block:(h + 1) * block]
+        sums = mul(inside, high) + mul(inside, low)
         for p in range(count):
-            part[p, :, cols(peers[d])] = sums[p * owned:(p + 1) * owned]
-
-    finish(0, conv_out.at[0])
-    for d in order[::-1]:
-        conv_sends[d].wait_recv()
-        finish(d, conv_in.at[d])
-
-    part_sends = {d: remote(part.at[peers[d]], part_in.at[d], send_p, recv_p, d) for d in order}
-    for d in order:
-        part_sends[d].start()
+            new = sums[p * owned:(p + 1) * owned]
+            part[p, :, at] = part[p, :, at] + new if h else new
+
+    skip_copy.wait()
+    for d in range(count):
+        if d:
+            sig_copies[d].wait()
+        gate_copies[d].wait()
+        for h in range(halves):
+            if d:
+                back_copy(d, h, peers[d]).wait_recv()
+            finish(d, h, conv_in if d else conv_out)
+
+    part_sends = [
+        remote(part.at[peers[d]], part_in.at[d], send_p.at[d], recv_p.at[d], peers[d]) for d in order
+    ]
+    for copy in part_sends:
+        copy.start()
     total = part[me]
-    for d in order:
-        part_sends[d].wait_recv()
+    for d, copy in zip(order, part_sends):
+        copy.wait_recv()
         total = total + part_in[d]
     pooled[...] = total / jnp.concatenate([sizes] * (width // LANES), axis=1).astype(jnp.float32)
 
     for copy in out_copies:
         copy.wait()
-    for group in (sig_sends, tap_sends, conv_sends, part_sends):
-        for d in order:
-            group[d].wait_send()
+    for copy in [*sig_sends.values(), *tap_sends.values(), *part_sends]:
+        copy.wait_send()
+    for d in order:
+        for h in range(halves):
+            back_copy(d, h, peers[d]).wait_send()
 
 
 def fits_kernel(tokens, width, count):
@@ -345,8 +388,8 @@
     forward, inverse = transform_tables(block)
     f32, bf16 = jnp.float32, jnp.bfloat16
     dma = pltpu.SemaphoreType.DMA
+    each = dma((count, halves))
     anywhere = pl.BlockSpec(memory_space=pl.ANY)
-    scalars = pl.BlockSpec(memory_space=pltpu.SMEM)
     vmem = pl.BlockSpec(memory_space=pltpu.VMEM)
     piece = pltpu.VMEM((count, tokens, lanes), f32)
     spectra = pltpu.VMEM((count * halves, 2 * block, lanes), f32)
@@ -356,24 +399,27 @@
             jax.ShapeDtypeStruct((tokens, width), f32),
             jax.ShapeDtypeStruct((owned, width), f32),
         ),
-        in_specs=[scalars, scalars, anywhere, anywhere, anywhere, vmem, anywhere, anywhere],
+        in_specs=[anywhere] * 8,
         out_specs=(anywhere, vmem),
         scratch_shapes=[
             piece, piece, piece, piece, spectra, spectra,
             pltpu.VMEM((count, 2 * block, halves * lanes), f32),
+            pltpu.VMEM((2 * block, lanes), f32),
             piece, piece, piece,
             pltpu.VMEM((segs, tokens), bf16),
             pltpu.VMEM((count, owned, width), f32),
             pltpu.VMEM((count, owned, width), f32),
             pltpu.VMEM(forward.shape, bf16),
             pltpu.VMEM(inverse.shape, bf16),
-            dma((count,)), dma((2,)), dma((count,)), dma,
-            dma((count,)), dma((count,)), dma((count,)), dma((count,)),
-            dma((count,)), dma((count,)), dma((count,)), dma((count,)),
-            dma((count,)),
+            pltpu.SMEM(lengths.shape, jnp.int32),
+            pltpu.SMEM(lengths.shape, jnp.int32),
+            pltpu.VMEM((1, width), f32),
+            dma((count,)), dma((5,)), dma((count,)), dma,
+            each, each, each, each, each, each,
+            dma((count,)), dma((count,)), each,
         ],
         compiler_params=pltpu.CompilerParams(
-            collective_id=0, has_side_effects=True, vmem_limit_bytes=40 * 1024 * 1024
+            collective_id=0, has_side_effects=True, vmem_limit_bytes=64 * 1024 * 1024
         ),
         name="mixer",
     )(

time: 58.8 us -> 55.1 us (0.937)
  local copies, waits for them, and re-layouts: 8.67 us -> 2.88 us
  Pallas kernels: 49.1 us -> 51.5 us
    unnamed x18 -> x4, local copies, waits for them, and re-layouts: 8.67 us -> 2.88 us
    pallas_call x1, Pallas kernels: 49.1 us -> 51.5 us  [fused_on_device(): pl.pallas_call(functools.partial(mixer_kernel, count, block), out_shape=(...]
where the time goes in v1:
time: 55.1 us; the launch traced here: 55 us
  Pallas kernels  51.5 us (93%)
  local copies, waits for them, and re-layouts  2.88 us (5%)
  between operations  0.65 us (1%)
    pallas_call x1, Pallas kernels, fused_on_device(): pl.pallas_call(functools.partial(mixer_kernel, count, block), out_shape=(...  51.5 us
    unnamed x4, local copies, waits for them, and re-layouts  2.88 us

profile of v1, /device:TPU:0, one launch (start us, length us, event | category | flops | bytes accessed | tf_op | source)
XLA Modules:
  0.0 55.0 jit_solution(1877351919362365434)
XLA Ops:
  0.6 51.5 %mixer.1 = (f32[512,512]{1,0:T(8,128)}, f32[8,512]{1,0:T(8,128)}) custom-call(s32[32]{0:T(128)} %lengths_at.1, s32[32]{0:T(128)} %rows_at.1, f32[512,512]{1,0:T(8,128)} %signal.1, f32[512,512]{1,0:T(8,128)} %taps.1, f32[512,512]{1,0:T(8,128)} %gate.1, f32[1,512]{1,0:T(1,128)} %bitcast.1, bf16[2,512,256]{2,1,0:T(8,128)(2,1)} %constant.4.clone.forward, ...), custom_call_target="tpu_custom_call" | custom-call | tf_op jit(solution)/shard_map/mixer/pallas_call | solution.py:396
  52.1 0.0 copy-start
  52.1 2.3 %copy.12 = f32[512,512]{1,0:T(8,128)} copy(f32[512,512]{1,0:T(8,128)} %get-tuple-element.4) | data formatting | bytes 2097152
  54.4 0.0 copy-done
  54.4 0.6 %copy.13 = f32[8,512]{1,0:T(8,128)} copy(f32[8,512]{1,0:T(8,128)S(1)} %copy-done) | data formatting | bytes 32768
Async XLA Ops:
  52.1 2.3 %copy-start = (f32[8,512]{1,0:T(8,128)S(1)}, f32[8,512]{1,0:T(8,128)}, u32[]{:S(2)}) copy-start(f32[8,512]{1,0:T(8,128)} %get-tuple-element.5) | copy-start | bytes 49156

commit v2 on v1

--- a/solution.py
+++ b/solution.py
@@ -156,7 +156,7 @@
     count, block,
     lengths_at, rows_at, signal, taps, gate, skip_at, forward, inverse,
     mixed, pooled,
-    sig_in, tap_in, sig_own, gate_own, spec_s, spec_h, prod, carry, conv_out, conv_in, mixed_v, member, part, part_in,
+    sig_in, tap_in, sig_own, gate_own, spec_s, spec_h, prod, acc, conv_out, conv_in, mixed_v, member, part, part_in,
     fwd_v, inv_v, lengths, rows, skip,
     local_sem, table_sem, gate_sem, tap_sem, send_s, recv_s, send_h, recv_h, send_c, recv_c, send_p, recv_p, out_sem,
 ):
@@ -219,8 +219,6 @@
     tap_sends = scatter(taps, tap_in, send_h, recv_h)
     for copy in sig_sends.values():
         copy.start()
-    for copy in tap_sends.values():
-        copy.start()
     inv_copy.start()
     skip_copy.start()
     for d in range(1, count):
@@ -245,58 +243,70 @@
 
     fwd_copy.wait()
 
-    def to_spectrum(source, place, spec):
-        value = source[...]
-        wide = jnp.concatenate([value[h * block:(h + 1) * block] for h in range(halves)], axis=1)
-        high, low = split_value(wide)
-        result = mul(fwd_v[0], high) + (mul(fwd_v[1], high) + mul(fwd_v[0], low))
-        for h in range(halves):
-            spec[place * halves + h] = result[:, h * lanes:(h + 1) * lanes]
+    def to_spectrum(source, index, spec):
+        high, low = split_value(source[...])
+        both = mul(fwd_v[0], jnp.concatenate([high, low], axis=1))
+        spec[index] = both[:, :lanes] + (both[:, lanes:] + mul(fwd_v[1], high))
 
     sig_copies[0].wait()
-    to_spectrum(sig_own.at[0], me, spec_s)
+    for h in range(halves):
+        to_spectrum(sig_own.at[0, pieces[h], :], me * halves + h, spec_s)
     tap_copy.wait()
-    to_spectrum(tap_in.at[0], me, spec_h)
-    for sends, source, spec in ((sig_sends, sig_in, spec_s), (tap_sends, tap_in, spec_h)):
-        for d in order[::-1]:
-            for h in range(halves):
-                sends[d, h].wait_recv()
-            to_spectrum(source.at[d], peers[d], spec)
-
-    def product_tile(sign, row, first, last):
-        re = pl.ds(pl.multiple_of(row, 8), 8)
-        im = pl.ds(pl.multiple_of(row + block, 8), 8)
-        s_re = [spec_s[i, re, :] for i in range(last)]
-        s_im = [spec_s[i, im, :] for i in range(last)]
-        h_re = [spec_h[i, re, :] for i in range(last)]
-        h_im = [spec_h[i, im, :] for i in range(last)]
-        old_re, old_im = (carry[re, :], carry[im, :]) if first else (None, None)
-        for j in range(first, last):
-            new_re = new_im = None
-            for i in range(j + 1):
-                k = j - i
-                a = s_re[i] * h_re[k] - s_im[i] * h_im[k]
-                b = s_re[i] * h_im[k] + s_im[i] * h_re[k]
-                new_re = a if new_re is None else new_re + a
-                new_im = b if new_im is None else new_im + b
-            out_re, out_im = new_re, new_im
-            if j:
-                out_re = new_re - old_im if sign > 0 else new_re + old_im
-                out_im = new_im + old_re if sign > 0 else new_im - old_re
-            at = pl.ds((j % halves) * lanes, lanes)
-            prod[j // halves, re, at] = out_re
-            prod[j // halves, im, at] = out_im
-            old_re, old_im = new_re, new_im
-        if last < blocks:
-            carry[re, :] = old_re
-            carry[im, :] = old_im
-
-    def products(first, last):
+    for h in range(halves):
+        to_spectrum(tap_in.at[0, pieces[h], :], me * halves + h, spec_h)
+    for h in range(halves):
+        for d in order:
+            sig_sends[d, h].wait_recv()
+            tap_sends[d, h].start()
+        for d in order:
+            to_spectrum(sig_in.at[d, pieces[h], :], peers[d] * halves + h, spec_s)
+
+    def take_taps(h):
+        for d in order:
+            tap_sends[d, h].wait_recv()
+            to_spectrum(tap_in.at[d, pieces[h], :], peers[d] * halves + h, spec_h)
+
+    def load(spec, wanted, re, im):
+        return {i: (spec[i, re, :], spec[i, im, :]) for i in wanted}
+
+    def products(first, last, lags, final):
+        def tile(sign, row):
+            re = pl.ds(pl.multiple_of(row, 8), 8)
+            im = pl.ds(pl.multiple_of(row + block, 8), 8)
+            used = [k for k in lags if k < last]
+            taps_at = load(spec_h, used, re, im)
+            sig_at = load(spec_s, sorted({j - k for j in range(first, last) for k in used if k <= j}), re, im)
+            old = (acc[first - 1, re, :], acc[first - 1, im, :]) if final and first else None
+            for j in range(first, last):
+                total = (acc[j, re, :], acc[j, im, :]) if final else None
+                for k in used:
+                    if k <= j:
+                        (a, b), (c, d) = sig_at[j - k], taps_at[k]
+                        new = (a * c - b * d, a * d + b * c)
+                        total = new if total is None else (total[0] + new[0], total[1] + new[1])
+                if not final:
+                    acc[j, re, :], acc[j, im, :] = total
+                    continue
+                out = total
+                if j:
+                    out = (total[0] - sign * old[1], total[1] + sign * old[0])
+                at = pl.ds((j % halves) * lanes, lanes)
+                prod[j // halves, re, at], prod[j // halves, im, at] = out
+                old = total
+            if final and last < blocks:
+                acc[last - 1, re, :], acc[last - 1, im, :] = old
+
         for sign, base in ((1, 0), (-1, block // 2)):
             def body(t, state, sign=sign, base=base):
-                product_tile(sign, base + t * 8, first, last)
+                tile(sign, base + t * 8)
                 return state
             lax.fori_loop(0, block // 16, body, 0)
+
+    for h in range(halves - 1):
+        take_taps(h)
+    products(0, blocks, [k for k in range(blocks) if k % halves < halves - 1], False)
+    take_taps(halves - 1)
+    late_lags = [k for k in range(blocks) if k % halves == halves - 1]
 
     def back_copy(d, h, peer):
         return remote(
@@ -316,10 +326,10 @@
                 back_copy(d, h, owner).start()
 
     inv_copy.wait()
-    products(0, blocks // 2)
+    products(0, blocks // 2, late_lags, True)
     for owner in range(count // 2):
         give_back(owner)
-    products(blocks // 2, blocks)
+    products(blocks // 2, blocks, late_lags, True)
     for owner in range(count // 2, count):
         give_back(owner)
 
@@ -374,7 +384,7 @@
         count > 1
         and count & (count - 1) == 0
         and width % (count * LANES) == 0
-        and tokens % (2 * LANES) == 0
+        and tokens % (4 * LANES) == 0
     )
 
 
@@ -404,7 +414,7 @@
         scratch_shapes=[
             piece, piece, piece, piece, spectra, spectra,
             pltpu.VMEM((count, 2 * block, halves * lanes), f32),
-            pltpu.VMEM((2 * block, lanes), f32),
+            spectra,
             piece, piece, piece,
             pltpu.VMEM((segs, tokens), bf16),
             pltpu.VMEM((count, owned, width), f32),

time: 55.1 us -> 53 us (0.962)
  Pallas kernels: 51.5 us -> 49.4 us
    pallas_call x1, Pallas kernels: 51.5 us -> 49.4 us  [fused_on_device(): pl.pallas_call(functools.partial(mixer_kernel, count, block), out_shape=(...]
where the time goes in v2:
time: 53 us; the launch traced here: 52.9 us
  Pallas kernels  49.4 us (93%)
  local copies, waits for them, and re-layouts  2.88 us (5%)
  between operations  0.65 us (1%)
    pallas_call x1, Pallas kernels, fused_on_device(): pl.pallas_call(functools.partial(mixer_kernel, count, block), out_shape=(...  49.4 us
    unnamed x4, local copies, waits for them, and re-layouts  2.88 us

profile of v2, /device:TPU:0, one launch (start us, length us, event | category | flops | bytes accessed | tf_op | source)
XLA Modules:
  0.0 52.9 jit_solution(1677004873173935154)
XLA Ops:
  0.6 49.4 %mixer.1 = (f32[512,512]{1,0:T(8,128)}, f32[8,512]{1,0:T(8,128)}) custom-call(s32[32]{0:T(128)} %lengths_at.1, s32[32]{0:T(128)} %rows_at.1, f32[512,512]{1,0:T(8,128)} %signal.1, f32[512,512]{1,0:T(8,128)} %taps.1, f32[512,512]{1,0:T(8,128)} %gate.1, f32[1,512]{1,0:T(1,128)} %bitcast.1, bf16[2,512,256]{2,1,0:T(8,128)(2,1)} %constant.4.clone.forward, ...), custom_call_target="tpu_custom_call" | custom-call | tf_op jit(solution)/shard_map/mixer/pallas_call | solution.py:406
  50.0 0.0 copy-start
  50.0 2.3 %copy.12 = f32[512,512]{1,0:T(8,128)} copy(f32[512,512]{1,0:T(8,128)} %get-tuple-element.4) | data formatting | bytes 2097152
  52.3 0.0 copy-done
  52.3 0.6 %copy.13 = f32[8,512]{1,0:T(8,128)} copy(f32[8,512]{1,0:T(8,128)S(1)} %copy-done) | data formatting | bytes 32768
Async XLA Ops:
  50.0 2.3 %copy-start = (f32[8,512]{1,0:T(8,128)S(1)}, f32[8,512]{1,0:T(8,128)}, u32[]{:S(2)}) copy-start(f32[8,512]{1,0:T(8,128)} %get-tuple-element.5) | copy-start | bytes 49156

commit v3 on v2

--- a/solution.py
+++ b/solution.py
@@ -11,6 +11,7 @@
 from jax.sharding import PartitionSpec as P
 
 LANES = 128
+STORES = 4
 MESH = pl.DeviceIdType.MESH
 
 exact_mode = lax.Precision.HIGHEST
@@ -152,6 +153,14 @@
     return peer
 
 
+class PeerOf:
+    def __init__(self, me, count):
+        self.me, self.count = me, count
+
+    def __getitem__(self, offset):
+        return peer_of(self.me, offset, self.count)
+
+
 def mixer_kernel(
     count, block,
     lengths_at, rows_at, signal, taps, gate, skip_at, forward, inverse,
@@ -161,13 +170,15 @@
     local_sem, table_sem, gate_sem, tap_sem, send_s, recv_s, send_h, recv_h, send_c, recv_c, send_p, recv_p, out_sem,
 ):
     me = lax.axis_index("seq")
+    core = lax.axis_index("chan") % 2
     tokens, width = signal.shape
     lanes = width // count
     halves = tokens // block
     blocks = halves * count
     owned = part.shape[1]
     segs = owned * count
-    peers = [peer_of(me, d, count) for d in range(count)]
+    order = [count - 1 - (e + core) % (count - 1) for e in range(count - 1)]
+    peers = PeerOf(me, count)
     pieces = [pl.ds(h * block, block) for h in range(halves)]
 
     def cols(index):
@@ -206,15 +217,14 @@
 
     def scatter(source, target, send, recv):
         return {
-            (d, h): remote(
+            (e, h): remote(
                 source.at[pieces[h], cols(peers[d])], target.at[d, pieces[h], :],
                 send.at[d, h], recv.at[d, h], peers[d],
             )
             for h in range(halves)
-            for d in order
+            for e, d in enumerate(order)
         }
 
-    order = list(range(count - 1, 0, -1))
     sig_sends = scatter(signal, sig_in, send_s, recv_s)
     tap_sends = scatter(taps, tap_in, send_h, recv_h)
     for copy in sig_sends.values():
@@ -255,15 +265,15 @@
     for h in range(halves):
         to_spectrum(tap_in.at[0, pieces[h], :], me * halves + h, spec_h)
     for h in range(halves):
-        for d in order:
-            sig_sends[d, h].wait_recv()
-            tap_sends[d, h].start()
+        for e in range(count - 1):
+            sig_sends[e, h].wait_recv()
+            tap_sends[e, h].start()
         for d in order:
             to_spectrum(sig_in.at[d, pieces[h], :], peers[d] * halves + h, spec_s)
 
     def take_taps(h):
-        for d in order:
-            tap_sends[d, h].wait_recv()
+        for e, d in enumerate(order):
+            tap_sends[e, h].wait_recv()
             to_spectrum(tap_in.at[d, pieces[h], :], peers[d] * halves + h, spec_h)
 
     def load(spec, wanted, re, im):
@@ -379,6 +389,17 @@
             back_copy(d, h, peers[d]).wait_send()
 
 
+def store_kernel(mixed_v, pooled_v, mixed, pooled, sem):
+    rows = mixed.shape[0] // STORES
+    parts = [pl.ds(i * rows, rows) for i in range(STORES)]
+    copies = [pltpu.make_async_copy(mixed_v.at[at, :], mixed.at[at, :], sem.at[i]) for i, at in enumerate(parts)]
+    copies.append(pltpu.make_async_copy(pooled_v, pooled, sem.at[STORES]))
+    for copy in copies:
+        copy.start()
+    for copy in copies:
+        copy.wait()
+
+
 def fits_kernel(tokens, width, count):
     return (
         count > 1
@@ -403,11 +424,11 @@
     vmem = pl.BlockSpec(memory_space=pltpu.VMEM)
     piece = pltpu.VMEM((count, tokens, lanes), f32)
     spectra = pltpu.VMEM((count * halves, 2 * block, lanes), f32)
-    return pl.pallas_call(
+    results = pl.pallas_call(
         functools.partial(mixer_kernel, count, block),
         out_shape=(
-            jax.ShapeDtypeStruct((tokens, width), f32),
-            jax.ShapeDtypeStruct((owned, width), f32),
+            pltpu.VMEM((tokens, width), f32),
+            pltpu.VMEM((owned, width), f32),
         ),
         in_specs=[anywhere] * 8,
         out_specs=(anywhere, vmem),
@@ -429,13 +450,22 @@
             dma((count,)), dma((count,)), each,
         ],
         compiler_params=pltpu.CompilerParams(
-            collective_id=0, has_side_effects=True, vmem_limit_bytes=64 * 1024 * 1024
+            collective_id=0, has_side_effects=True, vmem_limit_bytes=62 * 1024 * 1024
         ),
         name="mixer",
     )(
         lengths, row_of_segment, signal, filter_taps, out_gate, skip_gain[None, :],
         jnp.asarray(forward), jnp.asarray(inverse),
     )
+    return pl.pallas_call(
+        store_kernel,
+        out_shape=tuple(pltpu.HBM(result.shape, f32) for result in results),
+        in_specs=[anywhere] * 2,
+        out_specs=(anywhere,) * 2,
+        scratch_shapes=[dma((STORES + 1,))],
+        compiler_params=pltpu.CompilerParams(vmem_limit_bytes=1024 * 1024),
+        name="store",
+    )(*results)
 
 
 def on_device(signal, filter_taps, out_gate, skip_gain, lengths, row_of_segment):

time: 53 us -> 50.1 us (0.945)
  local copies, waits for them, and re-layouts: 2.88 us -> 0 us
    unnamed x4 -> x0, local copies, waits for them, and re-layouts: 2.88 us -> none
    pallas_call x1, Pallas kernels: 49.4 us -> 48.3 us  [fused_on_device(): pl.pallas_call(functools.partial(mixer_kernel, count, block), out_shape=(...]
    pallas_call x0 -> x1, Pallas kernels: none -> 1.01 us  [fused_on_device(): pl.pallas_call(store_kernel, out_shape=tuple((pltpu.HBM(result.shape, f32...]
where the time goes in v3:
time: 50.1 us; the launch traced here: 50 us
  Pallas kernels  49.3 us (98%)
  between operations  0.64 us (1%)
    pallas_call x1, Pallas kernels, fused_on_device(): pl.pallas_call(functools.partial(mixer_kernel, count, block), out_shape=(...  48.3 us
    pallas_call x1, Pallas kernels, fused_on_device(): pl.pallas_call(store_kernel, out_shape=tuple((pltpu.HBM(result.shape, f32...  1.01 us

profile of v3, /device:TPU:0, one launch (start us, length us, event | category | flops | bytes accessed | tf_op | source)
XLA Modules:
  0.0 50.0 jit_solution(10211018583984698557)
XLA Ops:
  0.6 48.3 %mixer.1 = (f32[512,512]{1,0:T(8,128)S(1)}, f32[8,512]{1,0:T(8,128)S(1)}) custom-call(s32[32]{0:T(128)} %lengths_at.1, s32[32]{0:T(128)} %rows_at.1, f32[512,512]{1,0:T(8,128)} %signal.1, f32[512,512]{1,0:T(8,128)} %taps.1, f32[512,512]{1,0:T(8,128)} %gate.1, f32[1,512]{1,0:T(1,128)} %bitcast.1, bf16[2,512,256]{2,1,0:T(8,128)(2,1)} %constant.4.clone.forward, ...), custom_call_target="tpu_custom_call" | custom-call | tf_op jit(solution)/shard_map/mixer/pallas_call | solution.py:427
  49.0 1.0 %store.1 = (f32[512,512]{1,0:T(8,128)}, f32[8,512]{1,0:T(8,128)}) custom-call(f32[512,512]{1,0:T(8,128)S(1)} %get-tuple-element.4.mixed_v, f32[8,512]{1,0:T(8,128)S(1)} %get-tuple-element.5.pooled_v), custom_call_target="tpu_custom_call" | custom-call | tf_op jit(solution)/shard_map/store/pallas_call | solution.py:460

commit v4 on v3

--- a/solution.py
+++ b/solution.py
@@ -177,7 +177,7 @@
     blocks = halves * count
     owned = part.shape[1]
     segs = owned * count
-    order = [count - 1 - (e + core) % (count - 1) for e in range(count - 1)]
+    order = [count - 1] + [1 + (e + core) % (count - 2) for e in range(count - 2)]
     peers = PeerOf(me, count)
     pieces = [pl.ds(h * block, block) for h in range(halves)]
 
@@ -323,25 +323,19 @@
             conv_out.at[d, pieces[h], :], conv_in.at[d, pieces[h], :], send_c.at[d, h], recv_c.at[d, h], peer
         )
 
-    def give_back(owner):
-        high, low = split_value(prod[owner])
+    def give_back(d):
+        high, low = split_value(prod[peers[d]])
         result = mul(inv_v[0], high) + (mul(inv_v[1], high) + mul(inv_v[0], low))
-        d = peer_of(me, owner, count)
         for h in range(halves):
             conv_out[d, pieces[h], :] = result[:, h * lanes:(h + 1) * lanes]
 
-        @pl.when(me != owner)
-        def _():
-            for h in range(halves):
-                back_copy(d, h, owner).start()
-
     inv_copy.wait()
-    products(0, blocks // 2, late_lags, True)
-    for owner in range(count // 2):
-        give_back(owner)
-    products(blocks // 2, blocks, late_lags, True)
-    for owner in range(count // 2, count):
-        give_back(owner)
+    products(0, blocks, late_lags, True)
+    for d in order:
+        give_back(d)
+        for h in range(halves):
+            back_copy(d, h, peers[d]).start()
+    give_back(0)
 
     out_copies = []
 
@@ -364,10 +358,12 @@
         if d:
             sig_copies[d].wait()
         gate_copies[d].wait()
+    for h in range(halves):
+        finish(0, h, conv_out)
+    for d in order:
         for h in range(halves):
-            if d:
-                back_copy(d, h, peers[d]).wait_recv()
-            finish(d, h, conv_in if d else conv_out)
+            back_copy(d, h, peers[d]).wait_recv()
+            finish(d, h, conv_in)
 
     part_sends = [
         remote(part.at[peers[d]], part_in.at[d], send_p.at[d], recv_p.at[d], peers[d]) for d in order

time: 50.1 us -> 49.6 us (0.990)
  no operation moved by 1% of the time
where the time goes in v4:
time: 49.6 us; the launch traced here: 49.5 us
  Pallas kernels  48.9 us (99%)
  between operations  0.64 us (1%)
    pallas_call x1, Pallas kernels, fused_on_device(): pl.pallas_call(functools.partial(mixer_kernel, count, block), out_shape=(...  47.8 us
    pallas_call x1, Pallas kernels, fused_on_device(): pl.pallas_call(store_kernel, out_shape=tuple((pltpu.HBM(result.shape, f32...  1.01 us

profile of v4, /device:TPU:0, one launch (start us, length us, event | category | flops | bytes accessed | tf_op | source)
XLA Modules:
  0.0 49.5 jit_solution(16632702343112499234)
XLA Ops:
  0.6 47.8 %mixer.1 = (f32[512,512]{1,0:T(8,128)S(1)}, f32[8,512]{1,0:T(8,128)S(1)}) custom-call(s32[32]{0:T(128)} %lengths_at.1, s32[32]{0:T(128)} %rows_at.1, f32[512,512]{1,0:T(8,128)} %signal.1, f32[512,512]{1,0:T(8,128)} %taps.1, f32[512,512]{1,0:T(8,128)} %gate.1, f32[1,512]{1,0:T(1,128)} %bitcast.1, bf16[2,512,256]{2,1,0:T(8,128)(2,1)} %constant.4.clone.forward, ...), custom_call_target="tpu_custom_call" | custom-call | tf_op jit(solution)/shard_map/mixer/pallas_call | solution.py:423
  48.5 1.0 %store.1 = (f32[512,512]{1,0:T(8,128)}, f32[8,512]{1,0:T(8,128)}) custom-call(f32[512,512]{1,0:T(8,128)S(1)} %get-tuple-element.4.mixed_v, f32[8,512]{1,0:T(8,128)S(1)} %get-tuple-element.5.pooled_v), custom_call_target="tpu_custom_call" | custom-call | tf_op jit(solution)/shard_map/store/pallas_call | solution.py:456

commit v5 on v4

--- a/solution.py
+++ b/solution.py
@@ -229,6 +229,8 @@
     tap_sends = scatter(taps, tap_in, send_h, recv_h)
     for copy in sig_sends.values():
         copy.start()
+    for e in range(count - 1):
+        tap_sends[e, 0].start()
     inv_copy.start()
     skip_copy.start()
     for d in range(1, count):
@@ -267,7 +269,8 @@
     for h in range(halves):
         for e in range(count - 1):
             sig_sends[e, h].wait_recv()
-            tap_sends[e, h].start()
+            if h + 1 < halves:
+                tap_sends[e, h + 1].start()
         for d in order:
             to_spectrum(sig_in.at[d, pieces[h], :], peers[d] * halves + h, spec_s)
 

time: 49.6 us -> 49.6 us (level)
  no operation moved by 1% of the time
where the time goes in v5:
time: 49.6 us; the launch traced here: 49.5 us
  Pallas kernels  48.9 us (99%)
  between operations  0.64 us (1%)
    pallas_call x1, Pallas kernels, fused_on_device(): pl.pallas_call(functools.partial(mixer_kernel, count, block), out_shape=(...  47.8 us
    pallas_call x1, Pallas kernels, fused_on_device(): pl.pallas_call(store_kernel, out_shape=tuple((pltpu.HBM(result.shape, f32...  1.01 us

profile of v5, /device:TPU:0, one launch (start us, length us, event | category | flops | bytes accessed | tf_op | source)
XLA Modules:
  0.0 49.5 jit_solution(5797361041749089148)
XLA Ops:
  0.6 47.8 %mixer.1 = (f32[512,512]{1,0:T(8,128)S(1)}, f32[8,512]{1,0:T(8,128)S(1)}) custom-call(s32[32]{0:T(128)} %lengths_at.1, s32[32]{0:T(128)} %rows_at.1, f32[512,512]{1,0:T(8,128)} %signal.1, f32[512,512]{1,0:T(8,128)} %taps.1, f32[512,512]{1,0:T(8,128)} %gate.1, f32[1,512]{1,0:T(1,128)} %bitcast.1, bf16[2,512,256]{2,1,0:T(8,128)(2,1)} %constant.4.clone.forward, ...), custom_call_target="tpu_custom_call" | custom-call | tf_op jit(solution)/shard_map/mixer/pallas_call | solution.py:426
  48.5 1.0 %store.1 = (f32[512,512]{1,0:T(8,128)}, f32[8,512]{1,0:T(8,128)}) custom-call(f32[512,512]{1,0:T(8,128)S(1)} %get-tuple-element.4.mixed_v, f32[8,512]{1,0:T(8,128)S(1)} %get-tuple-element.5.pooled_v), custom_call_target="tpu_custom_call" | custom-call | tf_op jit(solution)/shard_map/store/pallas_call | solution.py:459
